TPU v7x, 32 devices: a whole 2x2x4 slice. The times are simulated.
32 devices in a mesh: groups: 2 (over x), lib: 16 (over z, y, core).
Axes of the slice: x: 2, y: 2, z: 4, core: 2. Of those that a mesh axis runs over, the one named last changes fastest.
Arguments:
- spectra: bfloat16 [512, 4096], P(('groups', 'lib')), parts along dimension 0, may hold values from -6 to 6
- library: bfloat16 [8192, 4096], P('lib'), may hold values from -6 to 6
- cand_block: int32 [512, 8], P(('groups', 'lib')), parts along dimension 0, may hold values from 0 to 15, all different within a row; in each aligned block of 16 rows (0 to 15, 16 to 31, ...) at most 12 rows name the same one
- cand_local: int32 [512, 8, 8], P(('groups', 'lib')), parts along dimension 0, may hold values from 0 to 511
Outputs:
- profiles: float32 [512, 64, 1024], P(('groups', 'lib')), parts along dimension 0
There are 2 independent parts, one for each index of `groups`. A program takes and returns all parts, laid end to end along the dimension named above; an argument that names none is the same for every part. Nothing has to cross between parts.
Inputs may be any that keep to these rules, and one draw needn't show every extreme that they name: `cand_block`: each query names 8 different blocks; among the 16 queries of one device no block is named by more than 12 of them, and 12 is reached.
All inputs are finite; a program needn't handle non-finite values.
Results may differ from a plain program's by a relative error of at most 0.0029.
Values may be sent and summed in bfloat16 or wider, within the bound.
No kernel may reach another device: no remote copies, remote signals or barrier semaphores. Data moves between devices by JAX's collectives and lax.ppermute only.
A program may use at most 128 MiB of HBM per device.

v0:
```python
import functools

import jax
import jax.numpy as jnp
from jax import lax
from jax.experimental import pallas as pl
from jax.experimental.pallas import tpu as pltpu
from jax.sharding import PartitionSpec as P

SHIFTS = 1024
BG = 32
EPSILON = 1e-06
LANES = 128
VMEM_LIMIT = 48 * 1024 * 1024
NEAR = 4
ROW_SLOTS = 4
SLOT_LANES = LANES // ROW_SLOTS
PER_TOUCH = 8
CHAINS = 4
GROUPS = 4
WIDTH = LANES // GROUPS


def rounded(value, unit):
    return -(-value // unit) * unit


def depth_of(num_query, touches, devices):
    return min(num_query, max(3, 3 * num_query * touches // (2 * devices)))


def record_values(found):
    lane = lax.broadcasted_iota(jnp.int32, found.shape, 1) % SLOT_LANES
    low = pltpu.roll(found, LANES - PER_TOUCH, 1)
    return jnp.where(lane < PER_TOUCH, found * 16 + low, found).astype(jnp.int32)


def prepare_kernel(depth, spectra_ref, named_ref, wanted_ref, out_ref, table_ref, rows_ref):
    num_query, num_bins = spectra_ref.shape
    blocks = num_bins // LANES
    values = spectra_ref[...].astype(jnp.float32)
    zeros = jnp.zeros((num_query, LANES), jnp.float32)
    wide = jnp.concatenate([values, zeros], axis=1)
    total, length = wide, 1
    while length < 2 * BG:
        total = total + pltpu.roll(total, length, 1)
        length *= 2
    total = total + pltpu.roll(wide, length, 1)
    total = pltpu.roll(total, total.shape[1] - BG, 1)[:, :num_bins]
    centered = values - total / (2 * BG + 1)
    factor = lax.rsqrt(jnp.mean(centered * centered, axis=1, keepdims=True) + EPSILON)
    prepared = (centered * factor).astype(jnp.bfloat16)
    row = lax.broadcasted_iota(jnp.int32, (LANES, LANES), 0)
    col = lax.broadcasted_iota(jnp.int32, (LANES, LANES), 1)
    flip = jnp.where(row + col == LANES - 1, 1.0, 0.0).astype(jnp.bfloat16)
    for block in range(blocks):
        piece = prepared[:, block * LANES : (block + 1) * LANES]
        turned = jnp.dot(piece, flip, preferred_element_type=jnp.float32)
        rows_ref[pl.ds(blocks - 1 - block, num_query, stride=blocks), :] = turned
    out_ref[0 : num_query * blocks, :] = rows_ref[...].astype(jnp.bfloat16)

    touches = named_ref.shape[1]
    touched = num_query * touches
    records = table_ref.shape[0]
    per_block = rounded(depth, ROW_SLOTS) // ROW_SLOTS
    touch = lax.broadcasted_iota(jnp.int32, (touched, num_query), 0)
    query = lax.broadcasted_iota(jnp.int32, (touched, num_query), 1)
    owner = jnp.where(touch // touches == query, 1.0, 0.0).astype(jnp.bfloat16)
    named = named_ref[...].astype(jnp.float32).astype(jnp.bfloat16)
    spread = jnp.dot(owner, named, preferred_element_type=jnp.float32)
    touch = lax.broadcasted_iota(jnp.int32, (touched, touches), 0)
    which = lax.broadcasted_iota(jnp.int32, (touched, touches), 1)
    block_col = jnp.sum(
        jnp.where(touch % touches == which, spread, 0.0), axis=1, keepdims=True
    )
    row = lax.broadcasted_iota(jnp.int32, (touched, touched), 0)
    col = lax.broadcasted_iota(jnp.int32, (touched, touched), 1)
    block_row = jnp.sum(jnp.where(row == col, block_col, 0.0), axis=0, keepdims=True)
    earlier = (block_col == block_row) & (row < col)
    rank = jnp.sum(jnp.where(earlier, 1.0, 0.0), axis=0, keepdims=True).astype(jnp.int32)
    place = block_row.astype(jnp.int32) * per_block + rank // ROW_SLOTS
    wanted = wanted_ref[...]
    high = (wanted // 16).astype(jnp.float32).astype(jnp.bfloat16)
    low = (wanted % 16).astype(jnp.float32).astype(jnp.bfloat16)
    unit = lax.broadcasted_iota(jnp.int32, (PER_TOUCH, LANES), 0)
    lane = lax.broadcasted_iota(jnp.int32, (PER_TOUCH, LANES), 1)
    row = lax.broadcasted_iota(jnp.int32, (records, touched), 0)
    touch = lax.broadcasted_iota(jnp.int32, (touched, LANES), 0)
    wide_lane = lax.broadcasted_iota(jnp.int32, (touched, LANES), 1)
    found = jnp.zeros((records, LANES), jnp.float32)
    for group in range(ROW_SLOTS):
        start = group * SLOT_LANES
        to_high = jnp.where(lane == start + unit, 1.0, 0.0).astype(jnp.bfloat16)
        to_low = jnp.where(lane == start + PER_TOUCH + unit, 1.0, 0.0).astype(jnp.bfloat16)
        data = jnp.dot(high, to_high, preferred_element_type=jnp.float32)
        data = data + jnp.dot(low, to_low, preferred_element_type=jnp.float32)
        data = jnp.where(
            wide_lane == start + 2 * PER_TOUCH, (touch + 1).astype(jnp.float32), data
        ).astype(jnp.bfloat16)
        pick = jnp.where((row == place) & (rank % ROW_SLOTS == group), 1.0, 0.0)
        found = found + jnp.dot(
            pick.astype(jnp.bfloat16), data, preferred_element_type=jnp.float32
        )
    out_ref[num_query * blocks :, :] = found.astype(jnp.bfloat16)
    table_ref[...] = record_values(found)


def prepare(spectra, named, wanted, depth, records):
    num_query, num_bins = spectra.shape
    rows = num_query * num_bins // LANES
    return pl.pallas_call(
        functools.partial(prepare_kernel, depth),
        out_shape=(
            jax.ShapeDtypeStruct((rows + records, LANES), jnp.bfloat16),
            jax.ShapeDtypeStruct((records, LANES), jnp.int32),
        ),
        scratch_shapes=[pltpu.VMEM((rows, LANES), jnp.float32)],
        compiler_params=pltpu.CompilerParams(vmem_limit_bytes=VMEM_LIMIT),
        name="prepare",
    )(spectra, named, wanted)


def profile_kernel(depth, num_query, touches, me_ref, *refs):
    shards, library_ref, refs = refs[:NEAR], refs[NEAR], refs[NEAR + 1 :]
    outs, refs = refs[:NEAR], refs[NEAR:]
    query_ref, record_ref, found_ref, table_ref, order_ref, answer_ref, sem_ref = refs[:7]
    sets = [refs[7 + i :: 2] for i in range(2)]
    per_touch = PER_TOUCH
    rows = 2 * per_touch
    blocks = library_ref.shape[1]
    offsets = SHIFTS // LANES
    first = offsets // 2 + 1
    tiles = blocks // GROUPS
    query_rows = num_query * blocks
    per_block = rounded(depth, ROW_SLOTS) // ROW_SLOTS
    row = lax.broadcasted_iota(jnp.int32, (8, LANES), 0)
    lane = lax.broadcasted_iota(jnp.int32, (8, LANES), 1)
    lane16 = lax.broadcasted_iota(jnp.int32, (rows, LANES), 1)

    copies = [
        pltpu.make_async_copy(shards[e], query_ref.at[e], sem_ref.at[e]) for e in range(NEAR)
    ]
    for copy in copies:
        copy.start()
    for cand_ref, _, _, _, right_ref, _, _ in sets:
        cand_ref[...] = jnp.zeros(cand_ref.shape, cand_ref.dtype)
        right_ref[...] = jnp.zeros(right_ref.shape, right_ref.dtype)
    found_ref[...] = jnp.zeros(found_ref.shape, found_ref.dtype)
    for e in range(NEAR):
        copies[e].wait()
        record_ref[...] = query_ref[e, query_rows:, :].astype(jnp.float32)
        found_ref[e * per_block : (e + 1) * per_block, :] = record_values(
            record_ref[pl.ds(me_ref[0] * per_block, per_block), :]
        )
    to_scalars = pltpu.make_async_copy(found_ref, table_ref, sem_ref.at[NEAR])
    to_scalars.start()
    to_scalars.wait()

    def entry(slot):
        e = slot // depth
        s = slot % depth
        return e, e * per_block + s // ROW_SLOTS, s % ROW_SLOTS * SLOT_LANES

    def touch_of(slot):
        _, line, start = entry(slot)
        return table_ref[line, start + 2 * per_touch] - 1

    def choose(pieces):
        value = pieces[0]
        for group in range(1, GROUPS):
            value = jnp.where(lane16 < group * WIDTH, value, pieces[group])
        return value

    def gather(cand_ref, slot, half):
        _, line, start = entry(slot)
        for k in range(per_touch):
            wanted = table_ref[line, start + k]
            cand_ref[pl.ds(first * rows + half * per_touch + k, blocks, stride=rows), :] = (
                library_ref[wanted].astype(jnp.float32)
            )
        square = jnp.zeros((per_touch, LANES), jnp.float32)
        for b in range(blocks):
            piece = cand_ref[pl.ds((first + b) * rows + half * per_touch, per_touch), :]
            square = square + piece * piece
        mean = jnp.sum(square, axis=1, keepdims=True) / (blocks * LANES)
        return lax.rsqrt(mean + EPSILON)

    def make_left(cand_ref, packed_ref, left_ref):
        for b in range(blocks + offsets + 1):
            packed_ref[pl.ds(rows * b, rows), :] = cand_ref[pl.ds(rows * b, rows), :].astype(
                jnp.bfloat16
            )
        for t in range(tiles + offsets + 1):
            given = [packed_ref[pl.ds(rows * (t + tiles * g), rows), :] for g in range(GROUPS)]
            turned = []
            for c in range(GROUPS):
                mixed = choose([given[(a + c) % GROUPS] for a in range(GROUPS)])
                turned.append(pltpu.roll(mixed, WIDTH * c, 1) if c else mixed)
            for a in range(GROUPS):
                left_ref[a, pl.ds(rows * t, rows), :] = choose(
                    [turned[(g - a) % GROUPS] for g in range(GROUPS)]
                )

    def make_right(spectrum_ref, right_ref, slot, half):
        query = jnp.maximum(touch_of(slot), 0) // touches
        spectrum_ref[half] = query_ref[
            entry(slot)[0], pl.ds(pl.multiple_of(query * blocks, blocks), blocks), :
        ].astype(jnp.float32)
        zero = jnp.zeros((8, LANES), jnp.float32)
        before = (zero, zero)
        before_shifted = jnp.zeros((16, LANES), jnp.bfloat16)
        columns = slice(half * LANES, (half + 1) * LANES)
        for b in range(blocks + 1):
            if b < blocks:
                wide = jnp.broadcast_to(spectrum_ref[half, pl.ds(b, 1), :], (8, LANES))
                now = tuple(
                    pltpu.roll(wide, 1 + 8 * h, 1, stride=1, stride_axis=0) for h in range(2)
                )
            else:
                now = (zero, zero)
            shifted = jnp.concatenate(
                [jnp.where(lane > row + 8 * h, now[h], before[h]) for h in range(2)], axis=0
            ).astype(jnp.bfloat16)
            j = blocks - 1 - b
            place = 0 if j < 0 else (j % tiles + 1) * LANES + j // tiles * WIDTH
            right_ref[pl.ds(place, 16), columns] = shifted
            for c in range(16, WIDTH, 16):
                right_ref[pl.ds(place + c, 16), columns] = pltpu.roll(
                    jnp.where(lane16 < LANES - c, shifted, before_shifted), c, 1
                )
            before, before_shifted = now, shifted

    def sums(left_ref, right_ref, low, high):
        left = jnp.concatenate(
            [
                jnp.concatenate(
                    [
                        left_ref[a, pl.ds(rows * t, rows * (offsets + 1)), :]
                        for t in range(tiles + 1)
                    ],
                    axis=1,
                )
                for a in range(low, high)
            ],
            axis=0,
        )
        return jnp.dot(left, right_ref[...], preferred_element_type=jnp.float32)

    slots = NEAR * depth
    height = GROUPS // CHAINS * (offsets + 1) * rows

    step = GROUPS // CHAINS

    def make(pair, refs):
        cand_ref, packed_ref, spectrum_ref, left_ref, right_ref, scale_ref, _ = refs
        for half in range(2):
            scale_ref[half] = jnp.broadcast_to(
                gather(cand_ref, 2 * pair + half, half), (per_touch, LANES)
            )
        make_left(cand_ref, packed_ref, left_ref)
        for half in range(2):
            make_right(spectrum_ref, right_ref, 2 * pair + half, half)

    def finish(pair, refs):
        _, _, _, left_ref, right_ref, scale_ref, product_ref = refs
        for c in range(CHAINS):
            product_ref[c * height : (c + 1) * height, :] = sums(
                left_ref, right_ref, step * c, step * (c + 1)
            )

        def found(a, o, half):
            at = (a * (offsets + 1) + o) * rows + half * per_touch
            return product_ref[at : at + per_touch, half * LANES : (half + 1) * LANES]

        for o in range(offsets):
            both = []
            for half in range(2):
                total = found(0, o + 1, half)
                for a in range(1, GROUPS):
                    shift = WIDTH * a
                    total = total + pltpu.roll(
                        jnp.where(
                            lane < LANES - shift, found(a, o + 1, half), found(a, o, half)
                        ),
                        shift,
                        1,
                    )
                both.append(total * scale_ref[half])
            answer_ref[
                pl.ds(pl.multiple_of(16 * pair, 16), 16), o * LANES : (o + 1) * LANES
            ] = jnp.concatenate(both, axis=0).astype(jnp.bfloat16)

    order_ref[0] = 0

    def list_pair(pair, used):
        named = (touch_of(2 * pair) >= 0) | (touch_of(2 * pair + 1) >= 0)

        @pl.when(named)
        def _():
            for ahead in range(3):
                order_ref[used + ahead] = pair

        return used + named.astype(jnp.int32)

    used = lax.fori_loop(0, slots // 2, list_pair, jnp.int32(0))
    make(order_ref[0], sets[0])

    @pl.loop(0, (used + 1) // 2)
    def _(i):
        make(order_ref[2 * i + 1], sets[1])
        finish(order_ref[2 * i], sets[0])
        make(order_ref[2 * i + 2], sets[0])
        finish(order_ref[2 * i + 1], sets[1])

    back = [
        pltpu.make_async_copy(
            answer_ref.at[pl.ds(e * depth * per_touch, depth * per_touch), :],
            outs[e],
            sem_ref.at[e],
        )
        for e in range(NEAR)
    ]
    for copy in back:
        copy.start()
    for copy in back:
        copy.wait()


def profile(part, depth, num_query, touches, me, shards, library):
    blocks = library.shape[1]
    offsets = SHIFTS // LANES
    tiles = blocks // GROUPS
    records = shards[0].shape[0] - num_query * blocks
    per_block = rounded(depth, ROW_SLOTS) // ROW_SLOTS
    table = (rounded(NEAR * per_block, 8), LANES)
    smem = pl.BlockSpec(memory_space=pltpu.SMEM)
    vmem = pl.BlockSpec(memory_space=pltpu.VMEM)
    hbm = pl.BlockSpec(memory_space=pl.ANY)
    answers = NEAR * depth * PER_TOUCH
    flops = answers * 2 * (offsets + 1) * (blocks + 4) * LANES * LANES
    return pl.pallas_call(
        functools.partial(profile_kernel, depth, num_query, touches),
        out_shape=[
            jax.ShapeDtypeStruct((depth * PER_TOUCH, SHIFTS), jnp.bfloat16)
            for _ in range(NEAR)
        ],
        in_specs=[smem] + [hbm] * NEAR + [vmem],
        out_specs=[hbm] * NEAR,
        scratch_shapes=[
            pltpu.VMEM((NEAR, *shards[0].shape), jnp.bfloat16),
            pltpu.VMEM((records, LANES), jnp.float32),
            pltpu.VMEM(table, jnp.int32),
            pltpu.SMEM(table, jnp.int32),
            pltpu.SMEM((NEAR * depth // 2 + 3,), jnp.int32),
            pltpu.VMEM((answers, SHIFTS), jnp.bfloat16),
            pltpu.SemaphoreType.DMA((NEAR + 1,)),
        ]
        + [
            buffer
            for buffer in (
                pltpu.VMEM(((blocks + offsets + 1) * 16, LANES), jnp.float32),
                pltpu.VMEM(((blocks + offsets + 1) * 16, LANES), jnp.bfloat16),
                pltpu.VMEM((2, blocks, LANES), jnp.float32),
                pltpu.VMEM((GROUPS, (tiles + offsets + 1) * 16, LANES), jnp.bfloat16),
                pltpu.VMEM(((tiles + 1) * LANES, 2 * LANES), jnp.bfloat16),
                pltpu.VMEM((2, PER_TOUCH, LANES), jnp.float32),
                pltpu.VMEM((GROUPS * (offsets + 1) * 16, 2 * LANES), jnp.float32),
            )
            for _ in range(2)
        ],
        compiler_params=pltpu.CompilerParams(vmem_limit_bytes=VMEM_LIMIT),
        cost_estimate=pl.CostEstimate(
            flops=8 * flops, bytes_accessed=8 * 1024 * 1024, transcendentals=0
        ),
        name=f"profile_{part}",
    )(me, *shards, library)


def unpack_kernel(part, depth, me_ref, table_ref, *refs):
    got, refs = refs[:NEAR], refs[-3:]
    out_ref, stage_ref, sem_ref = refs
    per_block = rounded(depth, ROW_SLOTS) // ROW_SLOTS

    def copy(slot, touch):
        return pltpu.make_async_copy(stage_ref.at[slot], out_ref.at[touch], sem_ref.at[slot])

    def touch_of(e, s):
        block = jnp.bitwise_xor(me_ref[0], NEAR * part + e)
        line = block * per_block + s // ROW_SLOTS
        return table_ref[line, s % ROW_SLOTS * SLOT_LANES + 2 * PER_TOUCH] - 1

    for e in range(NEAR):
        for s in range(depth):
            touch = touch_of(e, s)
            slot = e * depth + s

            @pl.when(touch >= 0)
            def _():
                stage_ref[slot] = got[e][s * PER_TOUCH : (s + 1) * PER_TOUCH, :].astype(
                    jnp.float32
                )
                copy(slot, touch).start()

    for e in range(NEAR):
        for s in range(depth):
            touch = touch_of(e, s)

            @pl.when(touch >= 0)
            def _():
                copy(e * depth + s, touch).wait()


def unpack(part, depth, touched, me, table, got, out):
    shifts = got[0].shape[1]
    smem = pl.BlockSpec(memory_space=pltpu.SMEM)
    vmem = pl.BlockSpec(memory_space=pltpu.VMEM)
    hbm = pl.BlockSpec(memory_space=pl.ANY)
    more = () if out is None else (out,)
    return pl.pallas_call(
        functools.partial(unpack_kernel, part, depth),
        out_shape=jax.ShapeDtypeStruct((touched, PER_TOUCH, shifts), jnp.float32),
        in_specs=[smem] * 2 + [vmem] * NEAR + [hbm] * len(more),
        out_specs=hbm,
        scratch_shapes=[
            pltpu.VMEM((NEAR * depth, PER_TOUCH, shifts), jnp.float32),
            pltpu.SemaphoreType.DMA((NEAR * depth,)),
        ],
        input_output_aliases={2 + NEAR: 0} if more else {},
        compiler_params=pltpu.CompilerParams(vmem_limit_bytes=VMEM_LIMIT),
        cost_estimate=pl.CostEstimate(
            flops=0, bytes_accessed=NEAR * got[0].size * 6, transcendentals=0
        ),
        name=f"unpack_{part}",
    )(me, table, *got, *more)


def local(spectra, library, cand_block, cand_local):
    devices = lax.axis_size("lib")
    num_query, num_bins = spectra.shape
    touches, per_touch = cand_local.shape[1], cand_local.shape[2]
    depth = rounded(depth_of(num_query, touches, devices), 2)
    blocks = num_bins // LANES
    records = rounded(devices * (rounded(depth, ROW_SLOTS) // ROW_SLOTS), 16)
    me = lax.axis_index("lib").astype(jnp.int32).reshape(1)

    def across(value, distance):
        if distance == 0:
            return value
        pairs = [(i, i ^ distance) for i in range(devices)]
        return lax.ppermute(value, "lib", pairs)

    shard, table = prepare(
        spectra, cand_block, cand_local.reshape(-1, per_touch), depth, records
    )
    far = devices // NEAR
    order = [0] + list(range(far - 1, 0, -1))
    heads = {part: across(shard, NEAR * part) for part in order}
    shards = {
        part: [across(heads[part], e) for e in range(NEAR)] for part in order
    }
    rows = library.reshape(-1, blocks, LANES)
    got = {}
    for part in order:
        answers = profile(part, depth, num_query, touches, me, shards[part], rows)
        got[part] = [across(answers[e], NEAR * part + e) for e in range(NEAR)]
    out = None
    for part in order:
        out = unpack(part, depth, num_query * touches, me, table, got[part], out)
    return out.reshape(num_query, touches * per_touch, SHIFTS)


def solution(mesh):
    placed = (
        P(("groups", "lib"), None),
        P("lib", None),
        P(("groups", "lib"), None),
        P(("groups", "lib"), None, None),
    )
    return jax.shard_map(
        local,
        mesh=mesh,
        in_specs=placed,
        out_specs=P(("groups", "lib"), None, None),
        check_vma=False,
    )
```

profile of v0, /device:TPU:0, one launch (start us, length us, event | category | flops | bytes accessed | tf_op | source)
XLA Modules:
  0.0 238.4 jit_solution(2369808752331491049)
XLA Ops:
  0.0 0.8 copy.9.named_ref
  0.8 0.8 copy.8
  1.6 0.9 copy-done
  2.5 1.7 prepare.1
  4.2 2.5 %collective-permute-start.26 = (bf16[560,128]{1,0:T(8,128)(2,1)S(1)}, bf16[560,128]{1,0:T(8,128)(2,1)S(1)}, u32[]{:S(2)}, u32[]{:S(2)}) collective-permute-start(bf16[560,128]{1,0:T(8,128)(2,1)S(1)} %get-tuple-element.24.refs_0_), channel_id=1, source_target_pairs={{0,3},{1,2},{2,1},{3,0},{4,7},{5,6},{6,5},{7,4},{8,11},{9,10},{10,... | collective-permute-start | bytes 430088 | tf_op jit(solution)/shard_map/ppermute | solution.py:450
  6.7 3.6 %collective-permute-start.16 = (bf16[560,128]{1,0:T(8,128)(2,1)S(1)}, bf16[560,128]{1,0:T(8,128)(2,1)S(1)}, u32[]{:S(2)}, u32[]{:S(2)}) collective-permute-start(bf16[560,128]{1,0:T(8,128)(2,1)S(1)} %get-tuple-element.24.refs_0_), channel_id=1, source_target_pairs={{0,12},{1,13},{2,14},{3,15},{4,8},{5,9},{6,10},{7,11},{8,4},{9,5},... | collective-permute-start | bytes 430088 | tf_op jit(solution)/shard_map/ppermute | solution.py:450
  10.3 0.6 collective-permute-start.25
  10.9 3.5 %copy.10 = bf16[64,8,32,128]{3,2,1,0:T(8,128)(2,1)S(1)} copy(bf16[64,8,32,128]{3,1,2,0:T(8,128)(2,1)} %bitcast.10) | data formatting | bytes 8388608
  14.4 0.9 collective-permute-start
  15.3 0.9 collective-permute-start.19
  16.4 0.5 collective-permute-start.18
  17.2 6.2 %collective-permute-done.8.refs_0_ = bf16[560,128]{1,0:T(8,128)(2,1)S(1)} collective-permute-done((bf16[560,128]{1,0:T(8,128)(2,1)S(1)}, bf16[560,128]{1,0:T(8,128)(2,1)S(1)}, u32[]{:S(2)}, u32[]{:S(2)}) %collective-permute-start.8) | collective-permute-done | bytes 143392 | tf_op jit(solution)/shard_map/ppermute | solution.py:450
  23.4 27.7 %profile_0.1 = (bf16[96,1024]{1,0:T(8,128)(2,1)S(1)}, bf16[96,1024]{1,0:T(8,128)(2,1)S(1)}, bf16[96,1024]{1,0:T(8,128)(2,1)S(1)}, bf16[96,1024]{1,0:T(8,128)(2,1)S(1)}) custom-call(s32[1]{0:T(128)} %bitcast.me_ref, bf16[560,128]{1,0:T(8,128)(2,1)S(1)} %get-tuple-element.24.refs_0_, bf16[560,128]{1,0:T(8,128)(2,1)S(1)} %collective-permute-done.24.refs_1_, ...), custom_call_target="tpu_custom_call" | custom-call | flops 32614907904 | bytes 8388608 | tf_op jit(solution)/shard_map/profile_0/pallas_call | solution.py:341
  51.0 11.1 %collective-permute-start.10 = (bf16[560,128]{1,0:T(8,128)(2,1)S(1)}, bf16[560,128]{1,0:T(8,128)(2,1)S(1)}, u32[]{:S(2)}, u32[]{:S(2)}) collective-permute-start(bf16[560,128]{1,0:T(8,128)(2,1)S(1)} %collective-permute-done.8.refs_0_), channel_id=1, source_target_pairs={{0,2},{1,3},{2,0},{3,1},{4,6},{5,7},{6,4},{7,5},{8,10},{9,11},{10,... | collective-permute-start | bytes 430088 | tf_op jit(solution)/shard_map/ppermute | solution.py:450
  62.4 1.9 collective-permute-start.2
  64.3 27.6 %profile_3.1 = (bf16[96,1024]{1,0:T(8,128)(2,1)S(1)}, bf16[96,1024]{1,0:T(8,128)(2,1)S(1)}, bf16[96,1024]{1,0:T(8,128)(2,1)S(1)}, bf16[96,1024]{1,0:T(8,128)(2,1)S(1)}) custom-call(s32[1]{0:T(128)} %bitcast.me_ref, bf16[560,128]{1,0:T(8,128)(2,1)S(1)} %collective-permute-done.16.refs_0_, bf16[560,128]{1,0:T(8,128)(2,1)S(1)} %collective-permute-done.17.refs_1_, ...), custom_call_target="tpu_custom_call" | custom-call | flops 32614907904 | bytes 8388608 | tf_op jit(solution)/shard_map/profile_3/pallas_call | solution.py:341
  92.1 6.7 %collective-permute-start.28 = (bf16[96,1024]{1,0:T(8,128)(2,1)S(1)}, bf16[96,1024]{1,0:T(8,128)(2,1)S(1)}, u32[]{:S(2)}, u32[]{:S(2)}) collective-permute-start(bf16[96,1024]{1,0:T(8,128)(2,1)S(1)} %get-tuple-element.39), channel_id=1, source_target_pairs={{0,2},{1,3},{2,0},{3,1},{4,6},{5,7},{6,4},{7,5},{8,10},{9,11},{10,... | collective-permute-start | bytes 589832 | tf_op jit(solution)/shard_map/ppermute | solution.py:450
  98.9 19.1 %collective-permute-start.20 = (bf16[96,1024]{1,0:T(8,128)(2,1)S(1)}, bf16[96,1024]{1,0:T(8,128)(2,1)S(1)}, u32[]{:S(2)}, u32[]{:S(2)}) collective-permute-start(bf16[96,1024]{1,0:T(8,128)(2,1)S(1)} %get-tuple-element.33), channel_id=1, source_target_pairs={{0,12},{1,13},{2,14},{3,15},{4,8},{5,9},{6,10},{7,11},{8,4},{9,5},... | collective-permute-start | bytes 589832 | tf_op jit(solution)/shard_map/ppermute | solution.py:450
  118.1 27.6 %profile_2.1 = (bf16[96,1024]{1,0:T(8,128)(2,1)S(1)}, bf16[96,1024]{1,0:T(8,128)(2,1)S(1)}, bf16[96,1024]{1,0:T(8,128)(2,1)S(1)}, bf16[96,1024]{1,0:T(8,128)(2,1)S(1)}) custom-call(s32[1]{0:T(128)} %bitcast.me_ref, bf16[560,128]{1,0:T(8,128)(2,1)S(1)} %collective-permute-done.8.refs_0_, bf16[560,128]{1,0:T(8,128)(2,1)S(1)} %collective-permute-done.9.refs_1_, ...), custom_call_target="tpu_custom_call" | custom-call | flops 32614907904 | bytes 8388608 | tf_op jit(solution)/shard_map/profile_2/pallas_call | solution.py:341
  145.7 3.1 %collective-permute-start.22 = (bf16[96,1024]{1,0:T(8,128)(2,1)S(1)}, bf16[96,1024]{1,0:T(8,128)(2,1)S(1)}, u32[]{:S(2)}, u32[]{:S(2)}) collective-permute-start(bf16[96,1024]{1,0:T(8,128)(2,1)S(1)} %get-tuple-element.35), channel_id=1, source_target_pairs={{0,14},{1,15},{2,12},{3,13},{4,10},{5,11},{6,8},{7,9},{8,6},{9,7},... | collective-permute-start | bytes 589832 | tf_op jit(solution)/shard_map/ppermute | solution.py:450
  148.8 16.6 %collective-permute-start.12 = (bf16[96,1024]{1,0:T(8,128)(2,1)S(1)}, bf16[96,1024]{1,0:T(8,128)(2,1)S(1)}, u32[]{:S(2)}, u32[]{:S(2)}) collective-permute-start(bf16[96,1024]{1,0:T(8,128)(2,1)S(1)} %get-tuple-element.29), channel_id=1, source_target_pairs={{0,8},{1,9},{2,10},{3,11},{4,12},{5,13},{6,14},{7,15},{8,0},{9,1},... | collective-permute-start | bytes 589832 | tf_op jit(solution)/shard_map/ppermute | solution.py:450
  165.5 4.0 %collective-permute-start.14 = (bf16[96,1024]{1,0:T(8,128)(2,1)S(1)}, bf16[96,1024]{1,0:T(8,128)(2,1)S(1)}, u32[]{:S(2)}, u32[]{:S(2)}) collective-permute-start(bf16[96,1024]{1,0:T(8,128)(2,1)S(1)} %get-tuple-element.31), channel_id=1, source_target_pairs={{0,10},{1,11},{2,8},{3,9},{4,14},{5,15},{6,12},{7,13},{8,2},{9,3},... | collective-permute-start | bytes 589832 | tf_op jit(solution)/shard_map/ppermute | solution.py:450
  169.4 24.6 %profile_1.1 = (bf16[96,1024]{1,0:T(8,128)(2,1)S(1)}, bf16[96,1024]{1,0:T(8,128)(2,1)S(1)}, bf16[96,1024]{1,0:T(8,128)(2,1)S(1)}, bf16[96,1024]{1,0:T(8,128)(2,1)S(1)}) custom-call(s32[1]{0:T(128)} %bitcast.me_ref, bf16[560,128]{1,0:T(8,128)(2,1)S(1)} %collective-permute-done.refs_0_, bf16[560,128]{1,0:T(8,128)(2,1)S(1)} %collective-permute-done.1.refs_1_, ...), custom_call_target="tpu_custom_call" | custom-call | flops 32614907904 | bytes 8388608 | tf_op jit(solution)/shard_map/profile_1/pallas_call | solution.py:341
  194.0 19.2 %collective-permute-start.15 = (bf16[96,1024]{1,0:T(8,128)(2,1)S(1)}, bf16[96,1024]{1,0:T(8,128)(2,1)S(1)}, u32[]{:S(2)}, u32[]{:S(2)}) collective-permute-start(bf16[96,1024]{1,0:T(8,128)(2,1)S(1)} %get-tuple-element.32), channel_id=1, source_target_pairs={{0,11},{1,10},{2,9},{3,8},{4,15},{5,14},{6,13},{7,12},{8,3},{9,2},... | collective-permute-start | bytes 589832 | tf_op jit(solution)/shard_map/ppermute | solution.py:450
  213.3 6.3 %collective-permute-start.6 = (bf16[96,1024]{1,0:T(8,128)(2,1)S(1)}, bf16[96,1024]{1,0:T(8,128)(2,1)S(1)}, u32[]{:S(2)}, u32[]{:S(2)}) collective-permute-start(bf16[96,1024]{1,0:T(8,128)(2,1)S(1)} %get-tuple-element.27), channel_id=1, source_target_pairs={{0,6},{1,7},{2,4},{3,5},{4,2},{5,3},{6,0},{7,1},{8,14},{9,15},{10,... | collective-permute-start | bytes 589832 | tf_op jit(solution)/shard_map/ppermute | solution.py:450
  219.6 0.3 collective-permute-start.7
  219.9 2.6 %unpack_0.1.refs_4_ = f32[128,8,1024]{2,1,0:T(8,128)} custom-call(s32[1]{0:T(128)} %bitcast.me_ref, s32[48,128]{1,0:T(8,128)S(1)} %get-tuple-element.23.table_ref, bf16[96,1024]{1,0:T(8,128)(2,1)S(1)} %get-tuple-element.37.refs_0_, bf16[96,1024]{1,0:T(8,128)(2,1)S(1)} %collective-permute-done.27.refs_1_, ...), custom_call_target="tpu_custom_call" | custom-call | bytes 2359296 | tf_op jit(solution)/shard_map/unpack_0/pallas_call | solution.py:419
  222.5 2.6 %unpack_3.1.refs_4_ = f32[128,8,1024]{2,1,0:T(8,128)} custom-call(s32[1]{0:T(128)} %bitcast.me_ref, s32[48,128]{1,0:T(8,128)S(1)} %get-tuple-element.23.table_ref, bf16[96,1024]{1,0:T(8,128)(2,1)S(1)} %collective-permute-done.20.refs_0_, bf16[96,1024]{1,0:T(8,128)(2,1)S(1)} %collective-permute-done.21.refs_1_, ...), custom_call_target="tpu_custom_call", output_to_operand_aliasing={{}: (6, {})} | custom-call | bytes 2359296 | tf_op jit(solution)/shard_map/unpack_3/pallas_call | solution.py:419
  225.1 2.7 %unpack_2.1.refs_4_ = f32[128,8,1024]{2,1,0:T(8,128)} custom-call(s32[1]{0:T(128)} %bitcast.me_ref, s32[48,128]{1,0:T(8,128)S(1)} %get-tuple-element.23.table_ref, bf16[96,1024]{1,0:T(8,128)(2,1)S(1)} %collective-permute-done.12.refs_0_, bf16[96,1024]{1,0:T(8,128)(2,1)S(1)} %collective-permute-done.13.refs_1_, ...), custom_call_target="tpu_custom_call", output_to_operand_aliasing={{}: (6, {})} | custom-call | bytes 2359296 | tf_op jit(solution)/shard_map/unpack_2/pallas_call | solution.py:419
  227.8 4.4 %collective-permute-done.6.refs_2_ = bf16[96,1024]{1,0:T(8,128)(2,1)S(1)} collective-permute-done((bf16[96,1024]{1,0:T(8,128)(2,1)S(1)}, bf16[96,1024]{1,0:T(8,128)(2,1)S(1)}, u32[]{:S(2)}, u32[]{:S(2)}) %collective-permute-start.6) | collective-permute-done | bytes 196640 | tf_op jit(solution)/shard_map/ppermute | solution.py:450
  232.2 3.4 %collective-permute-done.7.refs_3_ = bf16[96,1024]{1,0:T(8,128)(2,1)S(1)} collective-permute-done((bf16[96,1024]{1,0:T(8,128)(2,1)S(1)}, bf16[96,1024]{1,0:T(8,128)(2,1)S(1)}, u32[]{:S(2)}, u32[]{:S(2)}) %collective-permute-start.7) | collective-permute-done | bytes 196640 | tf_op jit(solution)/shard_map/ppermute | solution.py:450
  235.6 2.7 %unpack_1.1 = f32[128,8,1024]{2,1,0:T(8,128)} custom-call(s32[1]{0:T(128)} %bitcast.me_ref, s32[48,128]{1,0:T(8,128)S(1)} %get-tuple-element.23.table_ref, bf16[96,1024]{1,0:T(8,128)(2,1)S(1)} %collective-permute-done.4.refs_0_, bf16[96,1024]{1,0:T(8,128)(2,1)S(1)} %collective-permute-done.5.refs_1_, ...), custom_call_target="tpu_custom_call", output_to_operand_aliasing={{}: (6, {})} | custom-call | bytes 2359296 | tf_op jit(solution)/shard_map/unpack_1/pallas_call | solution.py:419
  (42 shorter events, 1.1 us)
Async XLA Ops:
  1.6 0.9 copy-start
  4.2 10.2 %collective-permute-start.26 = (bf16[560,128]{1,0:T(8,128)(2,1)S(1)}, bf16[560,128]{1,0:T(8,128)(2,1)S(1)}, u32[]{:S(2)}, u32[]{:S(2)}) collective-permute-start(bf16[560,128]{1,0:T(8,128)(2,1)S(1)} %get-tuple-element.24.refs_0_), channel_id=1, source_target_pairs={{0,3},{1,2},{2,1},{3,0},{4,7},{5,6},{6,5},{7,4},{8,11},{9,10},{10,... | collective-permute-start | bytes 430088 | tf_op jit(solution)/shard_map/ppermute | solution.py:450
  6.7 8.6 %collective-permute-start.16 = (bf16[560,128]{1,0:T(8,128)(2,1)S(1)}, bf16[560,128]{1,0:T(8,128)(2,1)S(1)}, u32[]{:S(2)}, u32[]{:S(2)}) collective-permute-start(bf16[560,128]{1,0:T(8,128)(2,1)S(1)} %get-tuple-element.24.refs_0_), channel_id=1, source_target_pairs={{0,12},{1,13},{2,14},{3,15},{4,8},{5,9},{6,10},{7,11},{8,4},{9,5},... | collective-permute-start | bytes 430088 | tf_op jit(solution)/shard_map/ppermute | solution.py:450
  10.3 6.1 %collective-permute-start.25 = (bf16[560,128]{1,0:T(8,128)(2,1)S(1)}, bf16[560,128]{1,0:T(8,128)(2,1)S(1)}, u32[]{:S(2)}, u32[]{:S(2)}) collective-permute-start(bf16[560,128]{1,0:T(8,128)(2,1)S(1)} %get-tuple-element.24.refs_0_), channel_id=1, source_target_pairs={{0,2},{1,3},{2,0},{3,1},{4,6},{5,7},{6,4},{7,5},{8,10},{9,11},{10,... | collective-permute-start | bytes 430088 | tf_op jit(solution)/shard_map/ppermute | solution.py:450
  10.9 6.0 %collective-permute-start.24 = (bf16[560,128]{1,0:T(8,128)(2,1)S(1)}, bf16[560,128]{1,0:T(8,128)(2,1)S(1)}, u32[]{:S(2)}, u32[]{:S(2)}) collective-permute-start(bf16[560,128]{1,0:T(8,128)(2,1)S(1)} %get-tuple-element.24.refs_0_), channel_id=1, source_target_pairs={{0,1},{1,0},{2,3},{3,2},{4,5},{5,4},{6,7},{7,6},{8,9},{9,8},{10,11... | collective-permute-start | bytes 430088 | tf_op jit(solution)/shard_map/ppermute | solution.py:450
  10.9 12.4 %collective-permute-start.8 = (bf16[560,128]{1,0:T(8,128)(2,1)S(1)}, bf16[560,128]{1,0:T(8,128)(2,1)S(1)}, u32[]{:S(2)}, u32[]{:S(2)}) collective-permute-start(bf16[560,128]{1,0:T(8,128)(2,1)S(1)} %get-tuple-element.24.refs_0_), channel_id=1, source_target_pairs={{0,8},{1,9},{2,10},{3,11},{4,12},{5,13},{6,14},{7,15},{8,0},{9,1},... | collective-permute-start | bytes 430088 | tf_op jit(solution)/shard_map/ppermute | solution.py:450
  14.4 36.6 %collective-permute-start = (bf16[560,128]{1,0:T(8,128)(2,1)S(1)}, bf16[560,128]{1,0:T(8,128)(2,1)S(1)}, u32[]{:S(2)}, u32[]{:S(2)}) collective-permute-start(bf16[560,128]{1,0:T(8,128)(2,1)S(1)} %get-tuple-element.24.refs_0_), channel_id=1, source_target_pairs={{0,4},{1,5},{2,6},{3,7},{4,0},{5,1},{6,2},{7,3},{8,12},{9,13},{10,... | collective-permute-start | bytes 430088 | tf_op jit(solution)/shard_map/ppermute | solution.py:450
  15.3 46.9 %collective-permute-start.19 = (bf16[560,128]{1,0:T(8,128)(2,1)S(1)}, bf16[560,128]{1,0:T(8,128)(2,1)S(1)}, u32[]{:S(2)}, u32[]{:S(2)}) collective-permute-start(bf16[560,128]{1,0:T(8,128)(2,1)S(1)} %collective-permute-done.16.refs_0_), channel_id=1, source_target_pairs={{0,3},{1,2},{2,1},{3,0},{4,7},{5,6},{6,5},{7,4},{8,11},{9,10},{10,... | collective-permute-start | bytes 430088 | tf_op jit(solution)/shard_map/ppermute | solution.py:450
  16.4 45.8 %collective-permute-start.18 = (bf16[560,128]{1,0:T(8,128)(2,1)S(1)}, bf16[560,128]{1,0:T(8,128)(2,1)S(1)}, u32[]{:S(2)}, u32[]{:S(2)}) collective-permute-start(bf16[560,128]{1,0:T(8,128)(2,1)S(1)} %collective-permute-done.16.refs_0_), channel_id=1, source_target_pairs={{0,2},{1,3},{2,0},{3,1},{4,6},{5,7},{6,4},{7,5},{8,10},{9,11},{10,... | collective-permute-start | bytes 430088 | tf_op jit(solution)/shard_map/ppermute | solution.py:450
  16.9 45.5 %collective-permute-start.17 = (bf16[560,128]{1,0:T(8,128)(2,1)S(1)}, bf16[560,128]{1,0:T(8,128)(2,1)S(1)}, u32[]{:S(2)}, u32[]{:S(2)}) collective-permute-start(bf16[560,128]{1,0:T(8,128)(2,1)S(1)} %collective-permute-done.16.refs_0_), channel_id=1, source_target_pairs={{0,1},{1,0},{2,3},{3,2},{4,5},{5,4},{6,7},{7,6},{8,9},{9,8},{10,11... | collective-permute-start | bytes 430088 | tf_op jit(solution)/shard_map/ppermute | solution.py:450
  23.4 41.0 %collective-permute-start.11 = (bf16[560,128]{1,0:T(8,128)(2,1)S(1)}, bf16[560,128]{1,0:T(8,128)(2,1)S(1)}, u32[]{:S(2)}, u32[]{:S(2)}) collective-permute-start(bf16[560,128]{1,0:T(8,128)(2,1)S(1)} %collective-permute-done.8.refs_0_), channel_id=1, source_target_pairs={{0,3},{1,2},{2,1},{3,0},{4,7},{5,6},{6,5},{7,4},{8,11},{9,10},{10,... | collective-permute-start | bytes 430088 | tf_op jit(solution)/shard_map/ppermute | solution.py:450
  51.0 40.9 %collective-permute-start.10 = (bf16[560,128]{1,0:T(8,128)(2,1)S(1)}, bf16[560,128]{1,0:T(8,128)(2,1)S(1)}, u32[]{:S(2)}, u32[]{:S(2)}) collective-permute-start(bf16[560,128]{1,0:T(8,128)(2,1)S(1)} %collective-permute-done.8.refs_0_), channel_id=1, source_target_pairs={{0,2},{1,3},{2,0},{3,1},{4,6},{5,7},{6,4},{7,5},{8,10},{9,11},{10,... | collective-permute-start | bytes 430088 | tf_op jit(solution)/shard_map/ppermute | solution.py:450
  62.2 29.9 %collective-permute-start.9 = (bf16[560,128]{1,0:T(8,128)(2,1)S(1)}, bf16[560,128]{1,0:T(8,128)(2,1)S(1)}, u32[]{:S(2)}, u32[]{:S(2)}) collective-permute-start(bf16[560,128]{1,0:T(8,128)(2,1)S(1)} %collective-permute-done.8.refs_0_), channel_id=1, source_target_pairs={{0,1},{1,0},{2,3},{3,2},{4,5},{5,4},{6,7},{7,6},{8,9},{9,8},{10,11... | collective-permute-start | bytes 430088 | tf_op jit(solution)/shard_map/ppermute | solution.py:450
  62.2 36.6 %collective-permute-start.3 = (bf16[560,128]{1,0:T(8,128)(2,1)S(1)}, bf16[560,128]{1,0:T(8,128)(2,1)S(1)}, u32[]{:S(2)}, u32[]{:S(2)}) collective-permute-start(bf16[560,128]{1,0:T(8,128)(2,1)S(1)} %collective-permute-done.refs_0_), channel_id=1, source_target_pairs={{0,3},{1,2},{2,1},{3,0},{4,7},{5,6},{6,5},{7,4},{8,11},{9,10},{10,... | collective-permute-start | bytes 430088 | tf_op jit(solution)/shard_map/ppermute | solution.py:450
  62.4 36.5 %collective-permute-start.2 = (bf16[560,128]{1,0:T(8,128)(2,1)S(1)}, bf16[560,128]{1,0:T(8,128)(2,1)S(1)}, u32[]{:S(2)}, u32[]{:S(2)}) collective-permute-start(bf16[560,128]{1,0:T(8,128)(2,1)S(1)} %collective-permute-done.refs_0_), channel_id=1, source_target_pairs={{0,2},{1,3},{2,0},{3,1},{4,6},{5,7},{6,4},{7,5},{8,10},{9,11},{10,... | collective-permute-start | bytes 430088 | tf_op jit(solution)/shard_map/ppermute | solution.py:450
  64.3 53.7 %collective-permute-start.1 = (bf16[560,128]{1,0:T(8,128)(2,1)S(1)}, bf16[560,128]{1,0:T(8,128)(2,1)S(1)}, u32[]{:S(2)}, u32[]{:S(2)}) collective-permute-start(bf16[560,128]{1,0:T(8,128)(2,1)S(1)} %collective-permute-done.refs_0_), channel_id=1, source_target_pairs={{0,1},{1,0},{2,3},{3,2},{4,5},{5,4},{6,7},{7,6},{8,9},{9,8},{10,11... | collective-permute-start | bytes 430088 | tf_op jit(solution)/shard_map/ppermute | solution.py:450
  92.0 53.8 %collective-permute-start.27 = (bf16[96,1024]{1,0:T(8,128)(2,1)S(1)}, bf16[96,1024]{1,0:T(8,128)(2,1)S(1)}, u32[]{:S(2)}, u32[]{:S(2)}) collective-permute-start(bf16[96,1024]{1,0:T(8,128)(2,1)S(1)} %get-tuple-element.38), channel_id=1, source_target_pairs={{0,1},{1,0},{2,3},{3,2},{4,5},{5,4},{6,7},{7,6},{8,9},{9,8},{10,11... | collective-permute-start | bytes 589832 | tf_op jit(solution)/shard_map/ppermute | solution.py:450
  92.1 56.8 %collective-permute-start.28 = (bf16[96,1024]{1,0:T(8,128)(2,1)S(1)}, bf16[96,1024]{1,0:T(8,128)(2,1)S(1)}, u32[]{:S(2)}, u32[]{:S(2)}) collective-permute-start(bf16[96,1024]{1,0:T(8,128)(2,1)S(1)} %get-tuple-element.39), channel_id=1, source_target_pairs={{0,2},{1,3},{2,0},{3,1},{4,6},{5,7},{6,4},{7,5},{8,10},{9,11},{10,... | collective-permute-start | bytes 589832 | tf_op jit(solution)/shard_map/ppermute | solution.py:450
  98.8 50.1 %collective-permute-start.29 = (bf16[96,1024]{1,0:T(8,128)(2,1)S(1)}, bf16[96,1024]{1,0:T(8,128)(2,1)S(1)}, u32[]{:S(2)}, u32[]{:S(2)}) collective-permute-start(bf16[96,1024]{1,0:T(8,128)(2,1)S(1)} %get-tuple-element.40), channel_id=1, source_target_pairs={{0,3},{1,2},{2,1},{3,0},{4,7},{5,6},{6,5},{7,4},{8,11},{9,10},{10,... | collective-permute-start | bytes 589832 | tf_op jit(solution)/shard_map/ppermute | solution.py:450
  98.9 66.6 %collective-permute-start.20 = (bf16[96,1024]{1,0:T(8,128)(2,1)S(1)}, bf16[96,1024]{1,0:T(8,128)(2,1)S(1)}, u32[]{:S(2)}, u32[]{:S(2)}) collective-permute-start(bf16[96,1024]{1,0:T(8,128)(2,1)S(1)} %get-tuple-element.33), channel_id=1, source_target_pairs={{0,12},{1,13},{2,14},{3,15},{4,8},{5,9},{6,10},{7,11},{8,4},{9,5},... | collective-permute-start | bytes 589832 | tf_op jit(solution)/shard_map/ppermute | solution.py:450
  118.0 47.4 %collective-permute-start.21 = (bf16[96,1024]{1,0:T(8,128)(2,1)S(1)}, bf16[96,1024]{1,0:T(8,128)(2,1)S(1)}, u32[]{:S(2)}, u32[]{:S(2)}) collective-permute-start(bf16[96,1024]{1,0:T(8,128)(2,1)S(1)} %get-tuple-element.34), channel_id=1, source_target_pairs={{0,13},{1,12},{2,15},{3,14},{4,9},{5,8},{6,11},{7,10},{8,5},{9,4},... | collective-permute-start | bytes 589832 | tf_op jit(solution)/shard_map/ppermute | solution.py:450
  145.7 48.3 %collective-permute-start.22 = (bf16[96,1024]{1,0:T(8,128)(2,1)S(1)}, bf16[96,1024]{1,0:T(8,128)(2,1)S(1)}, u32[]{:S(2)}, u32[]{:S(2)}) collective-permute-start(bf16[96,1024]{1,0:T(8,128)(2,1)S(1)} %get-tuple-element.35), channel_id=1, source_target_pairs={{0,14},{1,15},{2,12},{3,13},{4,10},{5,11},{6,8},{7,9},{8,6},{9,7},... | collective-permute-start | bytes 589832 | tf_op jit(solution)/shard_map/ppermute | solution.py:450
  148.8 64.4 %collective-permute-start.23 = (bf16[96,1024]{1,0:T(8,128)(2,1)S(1)}, bf16[96,1024]{1,0:T(8,128)(2,1)S(1)}, u32[]{:S(2)}, u32[]{:S(2)}) collective-permute-start(bf16[96,1024]{1,0:T(8,128)(2,1)S(1)} %get-tuple-element.36), channel_id=1, source_target_pairs={{0,15},{1,14},{2,13},{3,12},{4,11},{5,10},{6,9},{7,8},{8,7},{9,6},... | collective-permute-start | bytes 589832 | tf_op jit(solution)/shard_map/ppermute | solution.py:450
  148.8 64.4 %collective-permute-start.12 = (bf16[96,1024]{1,0:T(8,128)(2,1)S(1)}, bf16[96,1024]{1,0:T(8,128)(2,1)S(1)}, u32[]{:S(2)}, u32[]{:S(2)}) collective-permute-start(bf16[96,1024]{1,0:T(8,128)(2,1)S(1)} %get-tuple-element.29), channel_id=1, source_target_pairs={{0,8},{1,9},{2,10},{3,11},{4,12},{5,13},{6,14},{7,15},{8,0},{9,1},... | collective-permute-start | bytes 589832 | tf_op jit(solution)/shard_map/ppermute | solution.py:450
  165.5 47.8 %collective-permute-start.13 = (bf16[96,1024]{1,0:T(8,128)(2,1)S(1)}, bf16[96,1024]{1,0:T(8,128)(2,1)S(1)}, u32[]{:S(2)}, u32[]{:S(2)}) collective-permute-start(bf16[96,1024]{1,0:T(8,128)(2,1)S(1)} %get-tuple-element.30), channel_id=1, source_target_pairs={{0,9},{1,8},{2,11},{3,10},{4,13},{5,12},{6,15},{7,14},{8,1},{9,0},... | collective-permute-start | bytes 589832 | tf_op jit(solution)/shard_map/ppermute | solution.py:450
  165.5 54.2 %collective-permute-start.14 = (bf16[96,1024]{1,0:T(8,128)(2,1)S(1)}, bf16[96,1024]{1,0:T(8,128)(2,1)S(1)}, u32[]{:S(2)}, u32[]{:S(2)}) collective-permute-start(bf16[96,1024]{1,0:T(8,128)(2,1)S(1)} %get-tuple-element.31), channel_id=1, source_target_pairs={{0,10},{1,11},{2,8},{3,9},{4,14},{5,15},{6,12},{7,13},{8,2},{9,3},... | collective-permute-start | bytes 589832 | tf_op jit(solution)/shard_map/ppermute | solution.py:450
  194.0 31.0 %collective-permute-start.15 = (bf16[96,1024]{1,0:T(8,128)(2,1)S(1)}, bf16[96,1024]{1,0:T(8,128)(2,1)S(1)}, u32[]{:S(2)}, u32[]{:S(2)}) collective-permute-start(bf16[96,1024]{1,0:T(8,128)(2,1)S(1)} %get-tuple-element.32), channel_id=1, source_target_pairs={{0,11},{1,10},{2,9},{3,8},{4,15},{5,14},{6,13},{7,12},{8,3},{9,2},... | collective-permute-start | bytes 589832 | tf_op jit(solution)/shard_map/ppermute | solution.py:450
  213.2 14.6 %collective-permute-start.4 = (bf16[96,1024]{1,0:T(8,128)(2,1)S(1)}, bf16[96,1024]{1,0:T(8,128)(2,1)S(1)}, u32[]{:S(2)}, u32[]{:S(2)}) collective-permute-start(bf16[96,1024]{1,0:T(8,128)(2,1)S(1)} %get-tuple-element.25), channel_id=1, source_target_pairs={{0,4},{1,5},{2,6},{3,7},{4,0},{5,1},{6,2},{7,3},{8,12},{9,13},{10,... | collective-permute-start | bytes 589832 | tf_op jit(solution)/shard_map/ppermute | solution.py:450
  213.2 14.6 %collective-permute-start.5 = (bf16[96,1024]{1,0:T(8,128)(2,1)S(1)}, bf16[96,1024]{1,0:T(8,128)(2,1)S(1)}, u32[]{:S(2)}, u32[]{:S(2)}) collective-permute-start(bf16[96,1024]{1,0:T(8,128)(2,1)S(1)} %get-tuple-element.26), channel_id=1, source_target_pairs={{0,5},{1,4},{2,7},{3,6},{4,1},{5,0},{6,3},{7,2},{8,13},{9,12},{10,... | collective-permute-start | bytes 589832 | tf_op jit(solution)/shard_map/ppermute | solution.py:450
  213.3 18.9 %collective-permute-start.6 = (bf16[96,1024]{1,0:T(8,128)(2,1)S(1)}, bf16[96,1024]{1,0:T(8,128)(2,1)S(1)}, u32[]{:S(2)}, u32[]{:S(2)}) collective-permute-start(bf16[96,1024]{1,0:T(8,128)(2,1)S(1)} %get-tuple-element.27), channel_id=1, source_target_pairs={{0,6},{1,7},{2,4},{3,5},{4,2},{5,3},{6,0},{7,1},{8,14},{9,15},{10,... | collective-permute-start | bytes 589832 | tf_op jit(solution)/shard_map/ppermute | solution.py:450
  219.6 15.9 %collective-permute-start.7 = (bf16[96,1024]{1,0:T(8,128)(2,1)S(1)}, bf16[96,1024]{1,0:T(8,128)(2,1)S(1)}, u32[]{:S(2)}, u32[]{:S(2)}) collective-permute-start(bf16[96,1024]{1,0:T(8,128)(2,1)S(1)} %get-tuple-element.28), channel_id=1, source_target_pairs={{0,7},{1,6},{2,5},{3,4},{4,3},{5,2},{6,1},{7,0},{8,15},{9,14},{10,... | collective-permute-start | bytes 589832 | tf_op jit(solution)/shard_map/ppermute | solution.py:450
where the time goes:
time: 240 us; the launch traced here: 238 us
  Pallas kernels  120 us (50%)
  starting transfers between devices  98.1 us (41%)
  waiting for transfers between devices  14.2 us (6%)
  local copies, waits for them, and re-layouts  5.95 us (2%)
    pallas_call x4, Pallas kernels, profile(): pl.pallas_call(functools.partial(profile_kernel, depth, num_query, touche...  108 us
    ppermute x30, starting transfers between devices, across(): return lax.ppermute(value, 'lib', pairs)  98.1 us
    ppermute x30, waiting for transfers between devices, across(): return lax.ppermute(value, 'lib', pairs)  14.2 us
    pallas_call x4, Pallas kernels, unpack(): pl.pallas_call(functools.partial(unpack_kernel, part, depth), out_shape=j...  10.5 us
    unnamed x5, local copies, waits for them, and re-layouts  5.95 us
  transfers between devices with their start and end apart: 30, of which 4 were waited for; matrix products, arithmetic and copies ran while one was open for 1% of the time, Pallas kernels for 48%

commit v1 on v0

--- a/solution.py
+++ b/solution.py
@@ -16,7 +16,7 @@
 ROW_SLOTS = 4
 SLOT_LANES = LANES // ROW_SLOTS
 PER_TOUCH = 8
-CHAINS = 4
+CHAINS = 2
 GROUPS = 4
 WIDTH = LANES // GROUPS
 
@@ -124,7 +124,8 @@
     shards, library_ref, refs = refs[:NEAR], refs[NEAR], refs[NEAR + 1 :]
     outs, refs = refs[:NEAR], refs[NEAR:]
     query_ref, record_ref, found_ref, table_ref, order_ref, answer_ref, sem_ref = refs[:7]
-    sets = [refs[7 + i :: 2] for i in range(2)]
+    cand_ref, packed_ref, spectrum_ref, product_ref = refs[7:11]
+    made, used_now = refs[11:14], refs[14:17]
     per_touch = PER_TOUCH
     rows = 2 * per_touch
     blocks = library_ref.shape[1]
@@ -142,9 +143,9 @@
     ]
     for copy in copies:
         copy.start()
-    for cand_ref, _, _, _, right_ref, _, _ in sets:
-        cand_ref[...] = jnp.zeros(cand_ref.shape, cand_ref.dtype)
-        right_ref[...] = jnp.zeros(right_ref.shape, right_ref.dtype)
+    cand_ref[...] = jnp.zeros(cand_ref.shape, cand_ref.dtype)
+    for ref in (*made, *used_now):
+        ref[...] = jnp.zeros(ref.shape, ref.dtype)
     found_ref[...] = jnp.zeros(found_ref.shape, found_ref.dtype)
     for e in range(NEAR):
         copies[e].wait()
@@ -251,8 +252,8 @@
 
     step = GROUPS // CHAINS
 
-    def make(pair, refs):
-        cand_ref, packed_ref, spectrum_ref, left_ref, right_ref, scale_ref, _ = refs
+    def make(pair):
+        left_ref, right_ref, scale_ref = made
         for half in range(2):
             scale_ref[half] = jnp.broadcast_to(
                 gather(cand_ref, 2 * pair + half, half), (per_touch, LANES)
@@ -261,8 +262,8 @@
         for half in range(2):
             make_right(spectrum_ref, right_ref, 2 * pair + half, half)
 
-    def finish(pair, refs):
-        _, _, _, left_ref, right_ref, scale_ref, product_ref = refs
+    def finish(pair):
+        left_ref, right_ref, scale_ref = used_now
         for c in range(CHAINS):
             product_ref[c * height : (c + 1) * height, :] = sums(
                 left_ref, right_ref, step * c, step * (c + 1)
@@ -303,14 +304,13 @@
         return used + named.astype(jnp.int32)
 
     used = lax.fori_loop(0, slots // 2, list_pair, jnp.int32(0))
-    make(order_ref[0], sets[0])
-
-    @pl.loop(0, (used + 1) // 2)
+
+    @pl.loop(0, used + 1)
     def _(i):
-        make(order_ref[2 * i + 1], sets[1])
-        finish(order_ref[2 * i], sets[0])
-        make(order_ref[2 * i + 2], sets[0])
-        finish(order_ref[2 * i + 1], sets[1])
+        for source, target in zip(made, used_now):
+            target[...] = source[...]
+        finish(order_ref[jnp.maximum(i - 1, 0)])
+        make(order_ref[i])
 
     back = [
         pltpu.make_async_copy(
@@ -356,18 +356,17 @@
             pltpu.SemaphoreType.DMA((NEAR + 1,)),
         ]
         + [
-            buffer
-            for buffer in (
-                pltpu.VMEM(((blocks + offsets + 1) * 16, LANES), jnp.float32),
-                pltpu.VMEM(((blocks + offsets + 1) * 16, LANES), jnp.bfloat16),
-                pltpu.VMEM((2, blocks, LANES), jnp.float32),
-                pltpu.VMEM((GROUPS, (tiles + offsets + 1) * 16, LANES), jnp.bfloat16),
-                pltpu.VMEM(((tiles + 1) * LANES, 2 * LANES), jnp.bfloat16),
-                pltpu.VMEM((2, PER_TOUCH, LANES), jnp.float32),
-                pltpu.VMEM((GROUPS * (offsets + 1) * 16, 2 * LANES), jnp.float32),
-            )
-            for _ in range(2)
-        ],
+            pltpu.VMEM(((blocks + offsets + 1) * 16, LANES), jnp.float32),
+            pltpu.VMEM(((blocks + offsets + 1) * 16, LANES), jnp.bfloat16),
+            pltpu.VMEM((2, blocks, LANES), jnp.float32),
+            pltpu.VMEM((GROUPS * (offsets + 1) * 16, 2 * LANES), jnp.float32),
+        ]
+        + [
+            pltpu.VMEM((GROUPS, (tiles + offsets + 1) * 16, LANES), jnp.bfloat16),
+            pltpu.VMEM(((tiles + 1) * LANES, 2 * LANES), jnp.bfloat16),
+            pltpu.VMEM((2, PER_TOUCH, LANES), jnp.float32),
+        ]
+        * 2,
         compiler_params=pltpu.CompilerParams(vmem_limit_bytes=VMEM_LIMIT),
         cost_estimate=pl.CostEstimate(
             flops=8 * flops, bytes_accessed=8 * 1024 * 1024, transcendentals=0

time: 240 us -> 245 us (1.021)
  Pallas kernels: 120 us -> 159 us
  starting transfers between devices: 98.1 us -> 63.2 us
    pallas_call x4, Pallas kernels: 108 us -> 147 us  [profile(): pl.pallas_call(functools.partial(profile_kernel, depth, num_query, touche...]
    ppermute x30, starting transfers between devices: 98.1 us -> 63.2 us  [across(): return lax.ppermute(value, 'lib', pairs)]
  transfers between devices with their start and end apart: 30 -> 30, of which waited for: 4 -> 5; matrix products, arithmetic and copies ran while one was open for 1% -> 1% of each run, Pallas kernels for 48% -> 63%
where the time goes in v1:
time: 245 us
  Pallas kernels  159 us (65%)
  starting transfers between devices  63.2 us (26%)
  waiting for transfers between devices  16.4 us (7%)
  local copies, waits for them, and re-layouts  5.95 us (2%)
    pallas_call x4, Pallas kernels, profile(): pl.pallas_call(functools.partial(profile_kernel, depth, num_query, touche...  147 us
    ppermute x30, starting transfers between devices, across(): return lax.ppermute(value, 'lib', pairs)  63.2 us
    ppermute x30, waiting for transfers between devices, across(): return lax.ppermute(value, 'lib', pairs)  16.4 us
    pallas_call x4, Pallas kernels, unpack(): pl.pallas_call(functools.partial(unpack_kernel, part, depth), out_shape=j...  10.5 us
    unnamed x5, local copies, waits for them, and re-layouts  5.95 us
  transfers between devices with their start and end apart: 30, of which 5 were waited for; matrix products, arithmetic and copies ran while one was open for 1% of the time, Pallas kernels for 63%

profile of v1, /device:TPU:0, one launch (start us, length us, event | category | flops | bytes accessed | tf_op | source)
XLA Modules:
  0.0 245.2 jit_solution(11963504299104381762)
XLA Ops:
  0.0 0.8 copy.9.named_ref
  0.8 0.8 copy.8
  1.6 0.9 copy-done
  2.5 1.7 prepare.1
  4.2 2.5 %collective-permute-start.26 = (bf16[560,128]{1,0:T(8,128)(2,1)S(1)}, bf16[560,128]{1,0:T(8,128)(2,1)S(1)}, u32[]{:S(2)}, u32[]{:S(2)}) collective-permute-start(bf16[560,128]{1,0:T(8,128)(2,1)S(1)} %get-tuple-element.24.refs_0_), channel_id=1, source_target_pairs={{0,3},{1,2},{2,1},{3,0},{4,7},{5,6},{6,5},{7,4},{8,11},{9,10},{10,... | collective-permute-start | bytes 430088 | tf_op jit(solution)/shard_map/ppermute | solution.py:449
  6.7 3.6 %collective-permute-start.16 = (bf16[560,128]{1,0:T(8,128)(2,1)S(1)}, bf16[560,128]{1,0:T(8,128)(2,1)S(1)}, u32[]{:S(2)}, u32[]{:S(2)}) collective-permute-start(bf16[560,128]{1,0:T(8,128)(2,1)S(1)} %get-tuple-element.24.refs_0_), channel_id=1, source_target_pairs={{0,12},{1,13},{2,14},{3,15},{4,8},{5,9},{6,10},{7,11},{8,4},{9,5},... | collective-permute-start | bytes 430088 | tf_op jit(solution)/shard_map/ppermute | solution.py:449
  10.9 3.5 %copy.10 = bf16[64,8,32,128]{3,2,1,0:T(8,128)(2,1)S(1)} copy(bf16[64,8,32,128]{3,1,2,0:T(8,128)(2,1)} %bitcast.10) | data formatting | bytes 8388608
  14.4 0.9 collective-permute-start
  15.3 0.9 collective-permute-start.19
  17.2 6.2 %collective-permute-done.8.refs_0_ = bf16[560,128]{1,0:T(8,128)(2,1)S(1)} collective-permute-done((bf16[560,128]{1,0:T(8,128)(2,1)S(1)}, bf16[560,128]{1,0:T(8,128)(2,1)S(1)}, u32[]{:S(2)}, u32[]{:S(2)}) %collective-permute-start.8) | collective-permute-done | bytes 143392 | tf_op jit(solution)/shard_map/ppermute | solution.py:449
  23.4 35.2 %profile_0.1 = (bf16[96,1024]{1,0:T(8,128)(2,1)S(1)}, bf16[96,1024]{1,0:T(8,128)(2,1)S(1)}, bf16[96,1024]{1,0:T(8,128)(2,1)S(1)}, bf16[96,1024]{1,0:T(8,128)(2,1)S(1)}) custom-call(s32[1]{0:T(128)} %bitcast.me_ref, bf16[560,128]{1,0:T(8,128)(2,1)S(1)} %get-tuple-element.24.refs_0_, bf16[560,128]{1,0:T(8,128)(2,1)S(1)} %collective-permute-done.24.refs_1_, ...), custom_call_target="tpu_custom_call" | custom-call | flops 32614907904 | bytes 8388608 | tf_op jit(solution)/shard_map/profile_0/pallas_call | solution.py:341
  58.5 11.3 %collective-permute-start.10 = (bf16[560,128]{1,0:T(8,128)(2,1)S(1)}, bf16[560,128]{1,0:T(8,128)(2,1)S(1)}, u32[]{:S(2)}, u32[]{:S(2)}) collective-permute-start(bf16[560,128]{1,0:T(8,128)(2,1)S(1)} %collective-permute-done.8.refs_0_), channel_id=1, source_target_pairs={{0,2},{1,3},{2,0},{3,1},{4,6},{5,7},{6,4},{7,5},{8,10},{9,11},{10,... | collective-permute-start | bytes 430088 | tf_op jit(solution)/shard_map/ppermute | solution.py:449
  70.1 1.9 collective-permute-start.2
  72.0 38.4 %profile_3.1 = (bf16[96,1024]{1,0:T(8,128)(2,1)S(1)}, bf16[96,1024]{1,0:T(8,128)(2,1)S(1)}, bf16[96,1024]{1,0:T(8,128)(2,1)S(1)}, bf16[96,1024]{1,0:T(8,128)(2,1)S(1)}) custom-call(s32[1]{0:T(128)} %bitcast.me_ref, bf16[560,128]{1,0:T(8,128)(2,1)S(1)} %collective-permute-done.16.refs_0_, bf16[560,128]{1,0:T(8,128)(2,1)S(1)} %collective-permute-done.17.refs_1_, ...), custom_call_target="tpu_custom_call" | custom-call | flops 32614907904 | bytes 8388608 | tf_op jit(solution)/shard_map/profile_3/pallas_call | solution.py:341
  110.5 3.9 %collective-permute-start.27 = (bf16[96,1024]{1,0:T(8,128)(2,1)S(1)}, bf16[96,1024]{1,0:T(8,128)(2,1)S(1)}, u32[]{:S(2)}, u32[]{:S(2)}) collective-permute-start(bf16[96,1024]{1,0:T(8,128)(2,1)S(1)} %get-tuple-element.38), channel_id=1, source_target_pairs={{0,1},{1,0},{2,3},{3,2},{4,5},{5,4},{6,7},{7,6},{8,9},{9,8},{10,11... | collective-permute-start | bytes 589832 | tf_op jit(solution)/shard_map/ppermute | solution.py:449
  114.3 3.0 %collective-permute-start.28 = (bf16[96,1024]{1,0:T(8,128)(2,1)S(1)}, bf16[96,1024]{1,0:T(8,128)(2,1)S(1)}, u32[]{:S(2)}, u32[]{:S(2)}) collective-permute-start(bf16[96,1024]{1,0:T(8,128)(2,1)S(1)} %get-tuple-element.39), channel_id=1, source_target_pairs={{0,2},{1,3},{2,0},{3,1},{4,6},{5,7},{6,4},{7,5},{8,10},{9,11},{10,... | collective-permute-start | bytes 589832 | tf_op jit(solution)/shard_map/ppermute | solution.py:449
  117.5 3.3 %collective-permute-start.21 = (bf16[96,1024]{1,0:T(8,128)(2,1)S(1)}, bf16[96,1024]{1,0:T(8,128)(2,1)S(1)}, u32[]{:S(2)}, u32[]{:S(2)}) collective-permute-start(bf16[96,1024]{1,0:T(8,128)(2,1)S(1)} %get-tuple-element.34), channel_id=1, source_target_pairs={{0,13},{1,12},{2,15},{3,14},{4,9},{5,8},{6,11},{7,10},{8,5},{9,4},... | collective-permute-start | bytes 589832 | tf_op jit(solution)/shard_map/ppermute | solution.py:449
  120.8 35.2 %profile_2.1 = (bf16[96,1024]{1,0:T(8,128)(2,1)S(1)}, bf16[96,1024]{1,0:T(8,128)(2,1)S(1)}, bf16[96,1024]{1,0:T(8,128)(2,1)S(1)}, bf16[96,1024]{1,0:T(8,128)(2,1)S(1)}) custom-call(s32[1]{0:T(128)} %bitcast.me_ref, bf16[560,128]{1,0:T(8,128)(2,1)S(1)} %collective-permute-done.8.refs_0_, bf16[560,128]{1,0:T(8,128)(2,1)S(1)} %collective-permute-done.9.refs_1_, ...), custom_call_target="tpu_custom_call" | custom-call | flops 32614907904 | bytes 8388608 | tf_op jit(solution)/shard_map/profile_2/pallas_call | solution.py:341
  156.1 14.6 %collective-permute-start.23 = (bf16[96,1024]{1,0:T(8,128)(2,1)S(1)}, bf16[96,1024]{1,0:T(8,128)(2,1)S(1)}, u32[]{:S(2)}, u32[]{:S(2)}) collective-permute-start(bf16[96,1024]{1,0:T(8,128)(2,1)S(1)} %get-tuple-element.36), channel_id=1, source_target_pairs={{0,15},{1,14},{2,13},{3,12},{4,11},{5,10},{6,9},{7,8},{8,7},{9,6},... | collective-permute-start | bytes 589832 | tf_op jit(solution)/shard_map/ppermute | solution.py:449
  170.7 4.0 %collective-permute-start.14 = (bf16[96,1024]{1,0:T(8,128)(2,1)S(1)}, bf16[96,1024]{1,0:T(8,128)(2,1)S(1)}, u32[]{:S(2)}, u32[]{:S(2)}) collective-permute-start(bf16[96,1024]{1,0:T(8,128)(2,1)S(1)} %get-tuple-element.31), channel_id=1, source_target_pairs={{0,10},{1,11},{2,8},{3,9},{4,14},{5,15},{6,12},{7,13},{8,2},{9,3},... | collective-permute-start | bytes 589832 | tf_op jit(solution)/shard_map/ppermute | solution.py:449
  174.8 38.4 %profile_1.1 = (bf16[96,1024]{1,0:T(8,128)(2,1)S(1)}, bf16[96,1024]{1,0:T(8,128)(2,1)S(1)}, bf16[96,1024]{1,0:T(8,128)(2,1)S(1)}, bf16[96,1024]{1,0:T(8,128)(2,1)S(1)}) custom-call(s32[1]{0:T(128)} %bitcast.me_ref, bf16[560,128]{1,0:T(8,128)(2,1)S(1)} %collective-permute-done.refs_0_, bf16[560,128]{1,0:T(8,128)(2,1)S(1)} %collective-permute-done.1.refs_1_, ...), custom_call_target="tpu_custom_call" | custom-call | flops 32614907904 | bytes 8388608 | tf_op jit(solution)/shard_map/profile_1/pallas_call | solution.py:341
  213.2 7.0 %collective-permute-start.15 = (bf16[96,1024]{1,0:T(8,128)(2,1)S(1)}, bf16[96,1024]{1,0:T(8,128)(2,1)S(1)}, u32[]{:S(2)}, u32[]{:S(2)}) collective-permute-start(bf16[96,1024]{1,0:T(8,128)(2,1)S(1)} %get-tuple-element.32), channel_id=1, source_target_pairs={{0,11},{1,10},{2,9},{3,8},{4,15},{5,14},{6,13},{7,12},{8,3},{9,2},... | collective-permute-start | bytes 589832 | tf_op jit(solution)/shard_map/ppermute | solution.py:449
  220.3 0.9 collective-permute-start.5
  221.1 0.7 collective-permute-start.6
  221.8 2.8 %collective-permute-start.7 = (bf16[96,1024]{1,0:T(8,128)(2,1)S(1)}, bf16[96,1024]{1,0:T(8,128)(2,1)S(1)}, u32[]{:S(2)}, u32[]{:S(2)}) collective-permute-start(bf16[96,1024]{1,0:T(8,128)(2,1)S(1)} %get-tuple-element.28), channel_id=1, source_target_pairs={{0,7},{1,6},{2,5},{3,4},{4,3},{5,2},{6,1},{7,0},{8,15},{9,14},{10,... | collective-permute-start | bytes 589832 | tf_op jit(solution)/shard_map/ppermute | solution.py:449
  224.7 2.6 %unpack_0.1.refs_4_ = f32[128,8,1024]{2,1,0:T(8,128)} custom-call(s32[1]{0:T(128)} %bitcast.me_ref, s32[48,128]{1,0:T(8,128)S(1)} %get-tuple-element.23.table_ref, bf16[96,1024]{1,0:T(8,128)(2,1)S(1)} %get-tuple-element.37.refs_0_, bf16[96,1024]{1,0:T(8,128)(2,1)S(1)} %collective-permute-done.27.refs_1_, ...), custom_call_target="tpu_custom_call" | custom-call | bytes 2359296 | tf_op jit(solution)/shard_map/unpack_0/pallas_call | solution.py:418
  227.3 2.6 %unpack_3.1.refs_4_ = f32[128,8,1024]{2,1,0:T(8,128)} custom-call(s32[1]{0:T(128)} %bitcast.me_ref, s32[48,128]{1,0:T(8,128)S(1)} %get-tuple-element.23.table_ref, bf16[96,1024]{1,0:T(8,128)(2,1)S(1)} %collective-permute-done.20.refs_0_, bf16[96,1024]{1,0:T(8,128)(2,1)S(1)} %collective-permute-done.21.refs_1_, ...), custom_call_target="tpu_custom_call", output_to_operand_aliasing={{}: (6, {})} | custom-call | bytes 2359296 | tf_op jit(solution)/shard_map/unpack_3/pallas_call | solution.py:418
  229.9 2.7 %unpack_2.1.refs_4_ = f32[128,8,1024]{2,1,0:T(8,128)} custom-call(s32[1]{0:T(128)} %bitcast.me_ref, s32[48,128]{1,0:T(8,128)S(1)} %get-tuple-element.23.table_ref, bf16[96,1024]{1,0:T(8,128)(2,1)S(1)} %collective-permute-done.12.refs_0_, bf16[96,1024]{1,0:T(8,128)(2,1)S(1)} %collective-permute-done.13.refs_1_, ...), custom_call_target="tpu_custom_call", output_to_operand_aliasing={{}: (6, {})} | custom-call | bytes 2359296 | tf_op jit(solution)/shard_map/unpack_2/pallas_call | solution.py:418
  232.6 1.4 collective-permute-done.5.refs_1_
  234.0 4.4 %collective-permute-done.6.refs_2_ = bf16[96,1024]{1,0:T(8,128)(2,1)S(1)} collective-permute-done((bf16[96,1024]{1,0:T(8,128)(2,1)S(1)}, bf16[96,1024]{1,0:T(8,128)(2,1)S(1)}, u32[]{:S(2)}, u32[]{:S(2)}) %collective-permute-start.6) | collective-permute-done | bytes 196640 | tf_op jit(solution)/shard_map/ppermute | solution.py:449
  238.4 4.1 %collective-permute-done.7.refs_3_ = bf16[96,1024]{1,0:T(8,128)(2,1)S(1)} collective-permute-done((bf16[96,1024]{1,0:T(8,128)(2,1)S(1)}, bf16[96,1024]{1,0:T(8,128)(2,1)S(1)}, u32[]{:S(2)}, u32[]{:S(2)}) %collective-permute-start.7) | collective-permute-done | bytes 196640 | tf_op jit(solution)/shard_map/ppermute | solution.py:449
  242.5 2.7 %unpack_1.1 = f32[128,8,1024]{2,1,0:T(8,128)} custom-call(s32[1]{0:T(128)} %bitcast.me_ref, s32[48,128]{1,0:T(8,128)S(1)} %get-tuple-element.23.table_ref, bf16[96,1024]{1,0:T(8,128)(2,1)S(1)} %collective-permute-done.4.refs_0_, bf16[96,1024]{1,0:T(8,128)(2,1)S(1)} %collective-permute-done.5.refs_1_, ...), custom_call_target="tpu_custom_call", output_to_operand_aliasing={{}: (6, {})} | custom-call | bytes 2359296 | tf_op jit(solution)/shard_map/unpack_1/pallas_call | solution.py:418
  (42 shorter events, 2.2 us)
Async XLA Ops:
  1.6 0.9 copy-start
  4.2 10.2 %collective-permute-start.26 = (bf16[560,128]{1,0:T(8,128)(2,1)S(1)}, bf16[560,128]{1,0:T(8,128)(2,1)S(1)}, u32[]{:S(2)}, u32[]{:S(2)}) collective-permute-start(bf16[560,128]{1,0:T(8,128)(2,1)S(1)} %get-tuple-element.24.refs_0_), channel_id=1, source_target_pairs={{0,3},{1,2},{2,1},{3,0},{4,7},{5,6},{6,5},{7,4},{8,11},{9,10},{10,... | collective-permute-start | bytes 430088 | tf_op jit(solution)/shard_map/ppermute | solution.py:449
  6.7 8.6 %collective-permute-start.16 = (bf16[560,128]{1,0:T(8,128)(2,1)S(1)}, bf16[560,128]{1,0:T(8,128)(2,1)S(1)}, u32[]{:S(2)}, u32[]{:S(2)}) collective-permute-start(bf16[560,128]{1,0:T(8,128)(2,1)S(1)} %get-tuple-element.24.refs_0_), channel_id=1, source_target_pairs={{0,12},{1,13},{2,14},{3,15},{4,8},{5,9},{6,10},{7,11},{8,4},{9,5},... | collective-permute-start | bytes 430088 | tf_op jit(solution)/shard_map/ppermute | solution.py:449
  10.3 6.1 %collective-permute-start.25 = (bf16[560,128]{1,0:T(8,128)(2,1)S(1)}, bf16[560,128]{1,0:T(8,128)(2,1)S(1)}, u32[]{:S(2)}, u32[]{:S(2)}) collective-permute-start(bf16[560,128]{1,0:T(8,128)(2,1)S(1)} %get-tuple-element.24.refs_0_), channel_id=1, source_target_pairs={{0,2},{1,3},{2,0},{3,1},{4,6},{5,7},{6,4},{7,5},{8,10},{9,11},{10,... | collective-permute-start | bytes 430088 | tf_op jit(solution)/shard_map/ppermute | solution.py:449
  10.9 6.0 %collective-permute-start.24 = (bf16[560,128]{1,0:T(8,128)(2,1)S(1)}, bf16[560,128]{1,0:T(8,128)(2,1)S(1)}, u32[]{:S(2)}, u32[]{:S(2)}) collective-permute-start(bf16[560,128]{1,0:T(8,128)(2,1)S(1)} %get-tuple-element.24.refs_0_), channel_id=1, source_target_pairs={{0,1},{1,0},{2,3},{3,2},{4,5},{5,4},{6,7},{7,6},{8,9},{9,8},{10,11... | collective-permute-start | bytes 430088 | tf_op jit(solution)/shard_map/ppermute | solution.py:449
  10.9 12.4 %collective-permute-start.8 = (bf16[560,128]{1,0:T(8,128)(2,1)S(1)}, bf16[560,128]{1,0:T(8,128)(2,1)S(1)}, u32[]{:S(2)}, u32[]{:S(2)}) collective-permute-start(bf16[560,128]{1,0:T(8,128)(2,1)S(1)} %get-tuple-element.24.refs_0_), channel_id=1, source_target_pairs={{0,8},{1,9},{2,10},{3,11},{4,12},{5,13},{6,14},{7,15},{8,0},{9,1},... | collective-permute-start | bytes 430088 | tf_op jit(solution)/shard_map/ppermute | solution.py:449
  14.4 44.1 %collective-permute-start = (bf16[560,128]{1,0:T(8,128)(2,1)S(1)}, bf16[560,128]{1,0:T(8,128)(2,1)S(1)}, u32[]{:S(2)}, u32[]{:S(2)}) collective-permute-start(bf16[560,128]{1,0:T(8,128)(2,1)S(1)} %get-tuple-element.24.refs_0_), channel_id=1, source_target_pairs={{0,4},{1,5},{2,6},{3,7},{4,0},{5,1},{6,2},{7,3},{8,12},{9,13},{10,... | collective-permute-start | bytes 430088 | tf_op jit(solution)/shard_map/ppermute | solution.py:449
  15.3 54.6 %collective-permute-start.19 = (bf16[560,128]{1,0:T(8,128)(2,1)S(1)}, bf16[560,128]{1,0:T(8,128)(2,1)S(1)}, u32[]{:S(2)}, u32[]{:S(2)}) collective-permute-start(bf16[560,128]{1,0:T(8,128)(2,1)S(1)} %collective-permute-done.16.refs_0_), channel_id=1, source_target_pairs={{0,3},{1,2},{2,1},{3,0},{4,7},{5,6},{6,5},{7,4},{8,11},{9,10},{10,... | collective-permute-start | bytes 430088 | tf_op jit(solution)/shard_map/ppermute | solution.py:449
  16.4 53.5 %collective-permute-start.18 = (bf16[560,128]{1,0:T(8,128)(2,1)S(1)}, bf16[560,128]{1,0:T(8,128)(2,1)S(1)}, u32[]{:S(2)}, u32[]{:S(2)}) collective-permute-start(bf16[560,128]{1,0:T(8,128)(2,1)S(1)} %collective-permute-done.16.refs_0_), channel_id=1, source_target_pairs={{0,2},{1,3},{2,0},{3,1},{4,6},{5,7},{6,4},{7,5},{8,10},{9,11},{10,... | collective-permute-start | bytes 430088 | tf_op jit(solution)/shard_map/ppermute | solution.py:449
  16.9 53.2 %collective-permute-start.17 = (bf16[560,128]{1,0:T(8,128)(2,1)S(1)}, bf16[560,128]{1,0:T(8,128)(2,1)S(1)}, u32[]{:S(2)}, u32[]{:S(2)}) collective-permute-start(bf16[560,128]{1,0:T(8,128)(2,1)S(1)} %collective-permute-done.16.refs_0_), channel_id=1, source_target_pairs={{0,1},{1,0},{2,3},{3,2},{4,5},{5,4},{6,7},{7,6},{8,9},{9,8},{10,11... | collective-permute-start | bytes 430088 | tf_op jit(solution)/shard_map/ppermute | solution.py:449
  23.4 48.7 %collective-permute-start.11 = (bf16[560,128]{1,0:T(8,128)(2,1)S(1)}, bf16[560,128]{1,0:T(8,128)(2,1)S(1)}, u32[]{:S(2)}, u32[]{:S(2)}) collective-permute-start(bf16[560,128]{1,0:T(8,128)(2,1)S(1)} %collective-permute-done.8.refs_0_), channel_id=1, source_target_pairs={{0,3},{1,2},{2,1},{3,0},{4,7},{5,6},{6,5},{7,4},{8,11},{9,10},{10,... | collective-permute-start | bytes 430088 | tf_op jit(solution)/shard_map/ppermute | solution.py:449
  58.5 51.9 %collective-permute-start.10 = (bf16[560,128]{1,0:T(8,128)(2,1)S(1)}, bf16[560,128]{1,0:T(8,128)(2,1)S(1)}, u32[]{:S(2)}, u32[]{:S(2)}) collective-permute-start(bf16[560,128]{1,0:T(8,128)(2,1)S(1)} %collective-permute-done.8.refs_0_), channel_id=1, source_target_pairs={{0,2},{1,3},{2,0},{3,1},{4,6},{5,7},{6,4},{7,5},{8,10},{9,11},{10,... | collective-permute-start | bytes 430088 | tf_op jit(solution)/shard_map/ppermute | solution.py:449
  69.9 44.5 %collective-permute-start.9 = (bf16[560,128]{1,0:T(8,128)(2,1)S(1)}, bf16[560,128]{1,0:T(8,128)(2,1)S(1)}, u32[]{:S(2)}, u32[]{:S(2)}) collective-permute-start(bf16[560,128]{1,0:T(8,128)(2,1)S(1)} %collective-permute-done.8.refs_0_), channel_id=1, source_target_pairs={{0,1},{1,0},{2,3},{3,2},{4,5},{5,4},{6,7},{7,6},{8,9},{9,8},{10,11... | collective-permute-start | bytes 430088 | tf_op jit(solution)/shard_map/ppermute | solution.py:449
  69.9 47.5 %collective-permute-start.3 = (bf16[560,128]{1,0:T(8,128)(2,1)S(1)}, bf16[560,128]{1,0:T(8,128)(2,1)S(1)}, u32[]{:S(2)}, u32[]{:S(2)}) collective-permute-start(bf16[560,128]{1,0:T(8,128)(2,1)S(1)} %collective-permute-done.refs_0_), channel_id=1, source_target_pairs={{0,3},{1,2},{2,1},{3,0},{4,7},{5,6},{6,5},{7,4},{8,11},{9,10},{10,... | collective-permute-start | bytes 430088 | tf_op jit(solution)/shard_map/ppermute | solution.py:449
  70.1 47.4 %collective-permute-start.2 = (bf16[560,128]{1,0:T(8,128)(2,1)S(1)}, bf16[560,128]{1,0:T(8,128)(2,1)S(1)}, u32[]{:S(2)}, u32[]{:S(2)}) collective-permute-start(bf16[560,128]{1,0:T(8,128)(2,1)S(1)} %collective-permute-done.refs_0_), channel_id=1, source_target_pairs={{0,2},{1,3},{2,0},{3,1},{4,6},{5,7},{6,4},{7,5},{8,10},{9,11},{10,... | collective-permute-start | bytes 430088 | tf_op jit(solution)/shard_map/ppermute | solution.py:449
  72.0 45.5 %collective-permute-start.1 = (bf16[560,128]{1,0:T(8,128)(2,1)S(1)}, bf16[560,128]{1,0:T(8,128)(2,1)S(1)}, u32[]{:S(2)}, u32[]{:S(2)}) collective-permute-start(bf16[560,128]{1,0:T(8,128)(2,1)S(1)} %collective-permute-done.refs_0_), channel_id=1, source_target_pairs={{0,1},{1,0},{2,3},{3,2},{4,5},{5,4},{6,7},{7,6},{8,9},{9,8},{10,11... | collective-permute-start | bytes 430088 | tf_op jit(solution)/shard_map/ppermute | solution.py:449
  110.5 45.5 %collective-permute-start.27 = (bf16[96,1024]{1,0:T(8,128)(2,1)S(1)}, bf16[96,1024]{1,0:T(8,128)(2,1)S(1)}, u32[]{:S(2)}, u32[]{:S(2)}) collective-permute-start(bf16[96,1024]{1,0:T(8,128)(2,1)S(1)} %get-tuple-element.38), channel_id=1, source_target_pairs={{0,1},{1,0},{2,3},{3,2},{4,5},{5,4},{6,7},{7,6},{8,9},{9,8},{10,11... | collective-permute-start | bytes 589832 | tf_op jit(solution)/shard_map/ppermute | solution.py:449
  114.3 41.7 %collective-permute-start.28 = (bf16[96,1024]{1,0:T(8,128)(2,1)S(1)}, bf16[96,1024]{1,0:T(8,128)(2,1)S(1)}, u32[]{:S(2)}, u32[]{:S(2)}) collective-permute-start(bf16[96,1024]{1,0:T(8,128)(2,1)S(1)} %get-tuple-element.39), channel_id=1, source_target_pairs={{0,2},{1,3},{2,0},{3,1},{4,6},{5,7},{6,4},{7,5},{8,10},{9,11},{10,... | collective-permute-start | bytes 589832 | tf_op jit(solution)/shard_map/ppermute | solution.py:449
  117.4 53.2 %collective-permute-start.29 = (bf16[96,1024]{1,0:T(8,128)(2,1)S(1)}, bf16[96,1024]{1,0:T(8,128)(2,1)S(1)}, u32[]{:S(2)}, u32[]{:S(2)}) collective-permute-start(bf16[96,1024]{1,0:T(8,128)(2,1)S(1)} %get-tuple-element.40), channel_id=1, source_target_pairs={{0,3},{1,2},{2,1},{3,0},{4,7},{5,6},{6,5},{7,4},{8,11},{9,10},{10,... | collective-permute-start | bytes 589832 | tf_op jit(solution)/shard_map/ppermute | solution.py:449
  117.5 53.1 %collective-permute-start.20 = (bf16[96,1024]{1,0:T(8,128)(2,1)S(1)}, bf16[96,1024]{1,0:T(8,128)(2,1)S(1)}, u32[]{:S(2)}, u32[]{:S(2)}) collective-permute-start(bf16[96,1024]{1,0:T(8,128)(2,1)S(1)} %get-tuple-element.33), channel_id=1, source_target_pairs={{0,12},{1,13},{2,14},{3,15},{4,8},{5,9},{6,10},{7,11},{8,4},{9,5},... | collective-permute-start | bytes 589832 | tf_op jit(solution)/shard_map/ppermute | solution.py:449
  117.5 53.2 %collective-permute-start.21 = (bf16[96,1024]{1,0:T(8,128)(2,1)S(1)}, bf16[96,1024]{1,0:T(8,128)(2,1)S(1)}, u32[]{:S(2)}, u32[]{:S(2)}) collective-permute-start(bf16[96,1024]{1,0:T(8,128)(2,1)S(1)} %get-tuple-element.34), channel_id=1, source_target_pairs={{0,13},{1,12},{2,15},{3,14},{4,9},{5,8},{6,11},{7,10},{8,5},{9,4},... | collective-permute-start | bytes 589832 | tf_op jit(solution)/shard_map/ppermute | solution.py:449
  156.0 57.2 %collective-permute-start.22 = (bf16[96,1024]{1,0:T(8,128)(2,1)S(1)}, bf16[96,1024]{1,0:T(8,128)(2,1)S(1)}, u32[]{:S(2)}, u32[]{:S(2)}) collective-permute-start(bf16[96,1024]{1,0:T(8,128)(2,1)S(1)} %get-tuple-element.35), channel_id=1, source_target_pairs={{0,14},{1,15},{2,12},{3,13},{4,10},{5,11},{6,8},{7,9},{8,6},{9,7},... | collective-permute-start | bytes 589832 | tf_op jit(solution)/shard_map/ppermute | solution.py:449
  156.1 64.2 %collective-permute-start.23 = (bf16[96,1024]{1,0:T(8,128)(2,1)S(1)}, bf16[96,1024]{1,0:T(8,128)(2,1)S(1)}, u32[]{:S(2)}, u32[]{:S(2)}) collective-permute-start(bf16[96,1024]{1,0:T(8,128)(2,1)S(1)} %get-tuple-element.36), channel_id=1, source_target_pairs={{0,15},{1,14},{2,13},{3,12},{4,11},{5,10},{6,9},{7,8},{8,7},{9,6},... | collective-permute-start | bytes 589832 | tf_op jit(solution)/shard_map/ppermute | solution.py:449
  170.6 49.7 %collective-permute-start.12 = (bf16[96,1024]{1,0:T(8,128)(2,1)S(1)}, bf16[96,1024]{1,0:T(8,128)(2,1)S(1)}, u32[]{:S(2)}, u32[]{:S(2)}) collective-permute-start(bf16[96,1024]{1,0:T(8,128)(2,1)S(1)} %get-tuple-element.29), channel_id=1, source_target_pairs={{0,8},{1,9},{2,10},{3,11},{4,12},{5,13},{6,14},{7,15},{8,0},{9,1},... | collective-permute-start | bytes 589832 | tf_op jit(solution)/shard_map/ppermute | solution.py:449
  170.6 50.5 %collective-permute-start.13 = (bf16[96,1024]{1,0:T(8,128)(2,1)S(1)}, bf16[96,1024]{1,0:T(8,128)(2,1)S(1)}, u32[]{:S(2)}, u32[]{:S(2)}) collective-permute-start(bf16[96,1024]{1,0:T(8,128)(2,1)S(1)} %get-tuple-element.30), channel_id=1, source_target_pairs={{0,9},{1,8},{2,11},{3,10},{4,13},{5,12},{6,15},{7,14},{8,1},{9,0},... | collective-permute-start | bytes 589832 | tf_op jit(solution)/shard_map/ppermute | solution.py:449
  170.7 51.1 %collective-permute-start.14 = (bf16[96,1024]{1,0:T(8,128)(2,1)S(1)}, bf16[96,1024]{1,0:T(8,128)(2,1)S(1)}, u32[]{:S(2)}, u32[]{:S(2)}) collective-permute-start(bf16[96,1024]{1,0:T(8,128)(2,1)S(1)} %get-tuple-element.31), channel_id=1, source_target_pairs={{0,10},{1,11},{2,8},{3,9},{4,14},{5,15},{6,12},{7,13},{8,2},{9,3},... | collective-permute-start | bytes 589832 | tf_op jit(solution)/shard_map/ppermute | solution.py:449
  213.2 16.7 %collective-permute-start.15 = (bf16[96,1024]{1,0:T(8,128)(2,1)S(1)}, bf16[96,1024]{1,0:T(8,128)(2,1)S(1)}, u32[]{:S(2)}, u32[]{:S(2)}) collective-permute-start(bf16[96,1024]{1,0:T(8,128)(2,1)S(1)} %get-tuple-element.32), channel_id=1, source_target_pairs={{0,11},{1,10},{2,9},{3,8},{4,15},{5,14},{6,13},{7,12},{8,3},{9,2},... | collective-permute-start | bytes 589832 | tf_op jit(solution)/shard_map/ppermute | solution.py:449
  220.3 12.3 %collective-permute-start.4 = (bf16[96,1024]{1,0:T(8,128)(2,1)S(1)}, bf16[96,1024]{1,0:T(8,128)(2,1)S(1)}, u32[]{:S(2)}, u32[]{:S(2)}) collective-permute-start(bf16[96,1024]{1,0:T(8,128)(2,1)S(1)} %get-tuple-element.25), channel_id=1, source_target_pairs={{0,4},{1,5},{2,6},{3,7},{4,0},{5,1},{6,2},{7,3},{8,12},{9,13},{10,... | collective-permute-start | bytes 589832 | tf_op jit(solution)/shard_map/ppermute | solution.py:449
  220.3 13.7 %collective-permute-start.5 = (bf16[96,1024]{1,0:T(8,128)(2,1)S(1)}, bf16[96,1024]{1,0:T(8,128)(2,1)S(1)}, u32[]{:S(2)}, u32[]{:S(2)}) collective-permute-start(bf16[96,1024]{1,0:T(8,128)(2,1)S(1)} %get-tuple-element.26), channel_id=1, source_target_pairs={{0,5},{1,4},{2,7},{3,6},{4,1},{5,0},{6,3},{7,2},{8,13},{9,12},{10,... | collective-permute-start | bytes 589832 | tf_op jit(solution)/shard_map/ppermute | solution.py:449
  221.1 17.3 %collective-permute-start.6 = (bf16[96,1024]{1,0:T(8,128)(2,1)S(1)}, bf16[96,1024]{1,0:T(8,128)(2,1)S(1)}, u32[]{:S(2)}, u32[]{:S(2)}) collective-permute-start(bf16[96,1024]{1,0:T(8,128)(2,1)S(1)} %get-tuple-element.27), channel_id=1, source_target_pairs={{0,6},{1,7},{2,4},{3,5},{4,2},{5,3},{6,0},{7,1},{8,14},{9,15},{10,... | collective-permute-start | bytes 589832 | tf_op jit(solution)/shard_map/ppermute | solution.py:449
  221.8 20.7 %collective-permute-start.7 = (bf16[96,1024]{1,0:T(8,128)(2,1)S(1)}, bf16[96,1024]{1,0:T(8,128)(2,1)S(1)}, u32[]{:S(2)}, u32[]{:S(2)}) collective-permute-start(bf16[96,1024]{1,0:T(8,128)(2,1)S(1)} %get-tuple-element.28), channel_id=1, source_target_pairs={{0,7},{1,6},{2,5},{3,4},{4,3},{5,2},{6,1},{7,0},{8,15},{9,14},{10,... | collective-permute-start | bytes 589832 | tf_op jit(solution)/shard_map/ppermute | solution.py:449
